TPU v7x, 512 devices: a whole 4x8x8 slice. The times are simulated.
512 devices in a mesh: leaf: 32 (over y, x), row: 8 (over z), col: 2 (over core).
Axes of the slice: x: 4, y: 8, z: 8, core: 2. Of those that a mesh axis runs over, the one named last changes fastest.
Arguments:
- leaf_update: float32 [32, 512, 512], P('leaf', 'row', 'col'), as said below
- leaf_rhs: float32 [32, 512, 256], P('leaf', 'row', 'col'), may hold values from -6 to 6
- child_rows: int32 [31, 2, 512], replicated, may hold values from 0 to 1023, as said below
- separator_coef: float32 [31, 512], replicated, may hold values from 0.5 to 4
Outputs:
- final_update: float32 [512, 512], P('row', 'col')
- final_rhs: float32 [512, 256], P('row', 'col')
- separator_solutions: float32 [32, 512, 256], P('leaf', 'row', 'col')
Inputs may be any that keep to these rules, and one draw needn't show every extreme that they name: Each child_rows[f, c] lists 512 distinct rows of the front. Each leaf_update[i] is symmetric positive definite.
All inputs are finite; a program needn't handle non-finite values.
Results may differ from a plain program's by a relative error of at most 0.00017.
Values sent between devices are 32-bit elements; how exact they have to be, the bound alone decides.
A program may use at most 128 MiB of HBM per device.

v0:
```python
import jax
import jax.numpy as jnp
from jax import lax
from jax.sharding import PartitionSpec as P


def from_partner(block, axis, apart):
    count = lax.axis_size(axis)
    route = []
    for low in range(count):
        high = low | 1 << apart
        if high != low and high < count:
            route += [(low, high), (high, low)]
    return lax.ppermute(block, axis, route)


def stencil_block(sep_coefs):
    positions = jnp.arange(sep_coefs.shape[0], dtype=jnp.int32)
    distance = positions[:, None] - positions[None, :]
    return jnp.where(
        distance == 0, sep_coefs[:, None] + 2.0, jnp.where(jnp.abs(distance) == 1, -1.0, 0.0)
    )


def matmul_high(left, right):
    return jnp.dot(left, right, precision=lax.Precision.HIGHEST)


def factor_inverse(matrix):
    order = matrix.shape[0]
    if order <= 32:
        lower_factor = jnp.linalg.cholesky(matrix)
        identity = jnp.eye(order, dtype=matrix.dtype)
        return jax.scipy.linalg.solve_triangular(lower_factor, identity, lower=True)
    half = order // 2
    inv_top = factor_inverse(matrix[:half, :half])
    lower_left = matmul_high(matrix[half:, :half], inv_top.T)
    schur_part = matrix[half:, half:] - matmul_high(lower_left, lower_left.T)
    inv_bottom = factor_inverse(schur_part)
    inv_left = -matmul_high(inv_bottom, matmul_high(lower_left, inv_top))
    upper_rows = jnp.concatenate([inv_top, jnp.zeros((half, order - half), matrix.dtype)], axis=1)
    lower_rows = jnp.concatenate([inv_left, inv_bottom], axis=1)
    return jnp.concatenate([upper_rows, lower_rows], axis=0)


def inverse_map(mapping, front_size):
    sources = jnp.arange(mapping.shape[0], dtype=jnp.int32)
    return jnp.full((front_size,), -1, jnp.int32).at[mapping].set(sources)


def spread_rows(full_rows, inverse, parent_rows):
    source = inverse[parent_rows]
    present = source >= 0
    picked = jnp.take(full_rows, jnp.maximum(source, 0), axis=0)
    return jnp.where(present[:, None], picked, 0.0)


def spread_block(full_matrix, inverse, parent_rows, parent_cols):
    src_rows = inverse[parent_rows]
    src_cols = inverse[parent_cols]
    picked = jnp.take(
        jnp.take(full_matrix, jnp.maximum(src_rows, 0), axis=0), jnp.maximum(src_cols, 0), axis=1
    )
    present = (src_rows >= 0)[:, None] & (src_cols >= 0)[None, :]
    return jnp.where(present, picked, 0.0)


def per_device(leaf_update, leaf_rhs, child_rows, separator_coef):
    update_blk = leaf_update[0]
    rhs_blk = leaf_rhs[0]
    leaf_count = lax.axis_size("leaf")
    row_count = lax.axis_size("row")
    col_count = lax.axis_size("col")
    levels = leaf_count.bit_length() - 1
    leaf_index = lax.axis_index("leaf")
    row_index = lax.axis_index("row")
    col_index = lax.axis_index("col")
    row_block, col_block = update_blk.shape
    rhs_cols = rhs_blk.shape[1]
    update_size = row_block * row_count
    sep_size = separator_coef.shape[1]
    front_size = sep_size + update_size
    sep_rows = jnp.arange(sep_size, dtype=jnp.int32)
    own_rows = sep_size + row_index * row_block + jnp.arange(row_block, dtype=jnp.int32)
    own_cols = sep_size + col_index * col_block + jnp.arange(col_block, dtype=jnp.int32)
    sep_share = sep_size // row_count
    kept_rows = jnp.zeros((sep_share, rhs_cols), jnp.float32)
    offset = 0
    for level_no in range(1, levels + 1):
        bit_no = level_no - 1
        other_upd, other_rhs = from_partner((update_blk, rhs_blk), "leaf", bit_no)
        blocks = lax.all_gather(
            jnp.stack([update_blk, other_upd])[:, None], ("row", "col"), axis=1, tiled=True
        )
        whole_rhs = lax.all_gather(jnp.stack([rhs_blk, other_rhs]), "row", axis=1, tiled=True)
        whole_upd = (
            blocks.reshape(2, row_count, col_count, row_block, col_block)
            .transpose(0, 1, 3, 2, 4)
            .reshape(2, update_size, update_size)
        )
        own_upd, partner_upd = (whole_upd[0], whole_upd[1])
        own_rhs, partner_rhs = (whole_rhs[0], whole_rhs[1])
        out_rows, out_cols = (own_rows, own_cols)
        upper_half = leaf_index >> bit_no & 1 == 1
        first_upd = jnp.where(upper_half, partner_upd, own_upd)
        second_upd = jnp.where(upper_half, own_upd, partner_upd)
        first_rhs = jnp.where(upper_half, partner_rhs, own_rhs)
        second_rhs = jnp.where(upper_half, own_rhs, partner_rhs)
        front_id = offset + (leaf_index >> level_no)
        mapping = lax.dynamic_index_in_dim(child_rows, front_id, 0, keepdims=False)
        sep_coefs = lax.dynamic_index_in_dim(separator_coef, front_id, 0, keepdims=False)
        inv_first = inverse_map(mapping[0], front_size)
        inv_second = inverse_map(mapping[1], front_size)

        def assemble(parent_rows, parent_cols):
            return spread_block(first_upd, inv_first, parent_rows, parent_cols) + spread_block(
                second_upd, inv_second, parent_rows, parent_cols
            )

        diag_block = stencil_block(sep_coefs) + assemble(sep_rows, sep_rows)
        factor_inv = factor_inverse(diag_block)
        panel_rows = matmul_high(factor_inv, assemble(out_rows, sep_rows).T)
        panel_cols = matmul_high(factor_inv, assemble(out_cols, sep_rows).T)
        update_blk = assemble(out_rows, out_cols) - matmul_high(panel_rows.T, panel_cols)
        rhs_sep = spread_rows(first_rhs, inv_first, sep_rows) + spread_rows(
            second_rhs, inv_second, sep_rows
        )
        rhs_own = spread_rows(first_rhs, inv_first, out_rows) + spread_rows(
            second_rhs, inv_second, out_rows
        )
        solved = matmul_high(factor_inv, rhs_sep)
        rhs_blk = rhs_own - matmul_high(panel_rows.T, solved)
        store_here = leaf_index & (1 << level_no) - 1 == 1 << bit_no
        if level_no == levels:
            store_here = store_here | (leaf_index & (1 << bit_no) - 1 == 0)
        kept_rows = jnp.where(
            store_here,
            lax.dynamic_slice_in_dim(solved, row_index * sep_share, sep_share, 0),
            kept_rows,
        )
        offset += leaf_count >> level_no
    return (update_blk, rhs_blk, kept_rows[None])


def solution(mesh):
    in_specs = (P("leaf", "row", "col"), P("leaf", "row", "col"), P(), P())
    out_specs = (P("row", "col"), P("row", "col"), P("leaf", "row", "col"))
    return jax.shard_map(
        per_device, mesh=mesh, in_specs=in_specs, out_specs=out_specs, check_vma=False
    )
```

profile of v0, /device:TPU:24, one launch (start us, length us, event | category | flops | bytes accessed | tf_op | source)
XLA Modules:
  0.0 1204.5 jit_solution(3808599444853935362)
XLA Ops:
  7.2 3.4 collective-permute-start
  35.0 27.9 %all-gather.11.cloned.1.call-done = f32[2,1024,256]{2,1,0:T(8,128)} async-done(((f32[2,64,256]{2,1,0:T(8,128)}), f32[2,1024,256]{2,1,0:T(8,128)}) %all-gather.11.cloned.1.call-update) | async-done | bytes 2097168 | tf_op jit(solution)/shard_map/all_gather | solution.py:92
  62.9 3.2 copy.566
  178.1 3.1 cholesky.1335
  225.3 4.9 collective-permute-start.1
  260.0 15.1 %all-gather.13.cloned.1.call-done = f32[2,1024,256]{2,1,0:T(8,128)} async-done(((f32[2,64,256]{2,1,0:T(8,128)}), f32[2,1024,256]{2,1,0:T(8,128)}) %all-gather.13.cloned.1.call-update) | async-done | bytes 2097168 | tf_op jit(solution)/shard_map/all_gather | solution.py:92
  391.3 3.1 cholesky.1511
  440.9 3.7 collective-permute-done.2
  445.3 3.4 collective-permute-start.5
  482.6 4.1 all-gather.15.cloned.1.call-done
  654.8 5.4 collective-permute-done.3
  674.6 26.3 %all_gather.35 = f32[2,512,128]{2,1,0:T(8,128)S(1)} all-gather(f32[2,64,128]{2,1,0:T(8,128)S(1)} %pad_maximum_fusion.5), channel_id=1, replica_groups=mesh['leaf'=32,'row'=8,'col'=2] {'row'}, dimensions={1}, use_global_device_ids=true | all-gather | bytes 589824 | tf_op jit(solution)/shard_map/all_gather | solution.py:95
  707.4 4.9 collective-permute-start.6
  827.7 3.3 cholesky.1863
  874.6 4.5 collective-permute-start.4
  879.9 5.5 collective-permute-done.4
  886.1 25.6 %all_gather.36 = f32[2,512,128]{2,1,0:T(8,128)S(1)} all-gather(f32[2,64,128]{2,1,0:T(8,128)S(1)} %pad_maximum_fusion.6), channel_id=1, replica_groups=mesh['leaf'=32,'row'=8,'col'=2] {'row'}, dimensions={1}, use_global_device_ids=true | all-gather | bytes 589824 | tf_op jit(solution)/shard_map/all_gather | solution.py:95
  919.1 3.9 collective-permute-done.7
  922.9 25.6 %all_gather.37 = f32[2,512,128]{2,1,0:T(8,128)S(1)} all-gather(f32[2,64,128]{2,1,0:T(8,128)S(1)} %pad_maximum_fusion.7), channel_id=1, replica_groups=mesh['leaf'=32,'row'=8,'col'=2] {'row'}, dimensions={1}, use_global_device_ids=true | all-gather | bytes 589824 | tf_op jit(solution)/shard_map/all_gather | solution.py:95
  955.9 4.8 collective-permute-done.8
  960.7 25.2 %all_gather.38 = f32[2,512,128]{2,1,0:T(8,128)S(1)} all-gather(f32[2,64,128]{2,1,0:T(8,128)S(1)} %pad_maximum_fusion.8), channel_id=1, replica_groups=mesh['leaf'=32,'row'=8,'col'=2] {'row'}, dimensions={1}, use_global_device_ids=true | all-gather | bytes 589824 | tf_op jit(solution)/shard_map/all_gather | solution.py:95
  991.5 4.6 collective-permute-start.9
  996.1 5.1 collective-permute-done.9
  1001.2 25.2 %all_gather.39 = f32[2,512,128]{2,1,0:T(8,128)S(1)} all-gather(f32[2,64,128]{2,1,0:T(8,128)S(1)} %pad_maximum_fusion.9), channel_id=1, replica_groups=mesh['leaf'=32,'row'=8,'col'=2] {'row'}, dimensions={1}, use_global_device_ids=true | all-gather | bytes 589824 | tf_op jit(solution)/shard_map/all_gather | solution.py:95
  (1954 shorter events, 939.3 us)
Async XLA Ops:
  7.2 55.7 %all-gather.11.cloned.1.call-start = ((), (), s32[]{:S(2)}) async-start(), calls=%async_computation | async-start | bytes 2228224 | tf_op jit(solution)/shard_map/all_gather | solution.py:92
  7.2 6.4 collective-permute-start
  15.1 259.9 %all-gather.13.cloned.1.call-start = ((), (), s32[]{:S(2)}) async-start(), calls=%async_computation.1 | async-start | bytes 2228224 | tf_op jit(solution)/shard_map/all_gather | solution.py:92
  31.0 181.2 %copy-start.89 = (s32[1024]{0:T(1024)}, s32[1024]{0:T(1024)S(1)}, u32[]{:S(2)}) copy-start(s32[1024]{0:T(1024)S(1)} %pad_clamp_fusion.24) | copy-start | bytes 12292
  31.7 178.6 %copy-start.91 = (s32[1024]{0:T(1024)}, s32[1024]{0:T(1024)S(1)}, u32[]{:S(2)}) copy-start(s32[1024]{0:T(1024)S(1)} %pad_clamp_fusion.25) | copy-start | bytes 12292
  153.4 69.9 %copy-start.25 = (f32[256,256]{1,0:T(8,128)}, f32[256,256]{1,0:T(8,128)S(1)}, u32[]{:S(2)}) copy-start(f32[256,256]{1,0:T(8,128)S(1)} %select_maximum_fusion.9) | copy-start | bytes 786436
  154.9 54.8 %copy-start.24 = (f32[256,64]{1,0:T(8,128)S(1)}, f32[256,64]{1,0:T(8,128)}, u32[]{:S(2)}) copy-start(f32[256,64]{1,0:T(8,128)} %gather_fusion.33) | copy-start | bytes 196612
  225.3 7.7 collective-permute-start.1
  233.6 253.1 %all-gather.15.cloned.1.call-start = ((), (), s32[]{:S(2)}) async-start(), calls=%async_computation.2 | async-start | bytes 2228224 | tf_op jit(solution)/shard_map/all_gather | solution.py:92
  256.3 169.2 %copy-start.93 = (s32[1024]{0:T(1024)}, s32[1024]{0:T(1024)S(1)}, u32[]{:S(2)}) copy-start(s32[1024]{0:T(1024)S(1)} %pad_clamp_fusion.18) | copy-start | bytes 12292
  365.8 70.8 %copy-start.27 = (f32[256,256]{1,0:T(8,128)}, f32[256,256]{1,0:T(8,128)S(1)}, u32[]{:S(2)}) copy-start(f32[256,256]{1,0:T(8,128)S(1)} %select_maximum_fusion.8) | copy-start | bytes 786436
  368.0 55.0 %copy-start.18 = (f32[256,64]{1,0:T(8,128)S(1)}, f32[256,64]{1,0:T(8,128)}, u32[]{:S(2)}) copy-start(f32[256,64]{1,0:T(8,128)} %gather_fusion.45) | copy-start | bytes 196612
  438.4 6.2 collective-permute-start.2
  445.3 267.1 %all-gather.17.cloned.1.call-start = ((), (), s32[]{:S(2)}) async-start(), calls=%async_computation.3 | async-start | bytes 2228224 | tf_op jit(solution)/shard_map/all_gather | solution.py:92
  445.3 228.5 %collective-permute-start.5 = (f32[64,128]{1,0:T(8,128)}, f32[64,128]{1,0:T(8,128)}, u32[]{:S(2)}, u32[]{:S(2)}) collective-permute-start(f32[64,128]{1,0:T(8,128)} %bitcast.331), channel_id=1, source_target_pairs={{0,16},{16,0},{32,48},{48,32},{64,80},{80,64},{96,112},{112,96},{1... | collective-permute-start | bytes 98312 | tf_op jit(solution)/shard_map/ppermute | solution.py:14
  578.6 71.3 %copy-start.29 = (f32[256,256]{1,0:T(8,128)}, f32[256,256]{1,0:T(8,128)S(1)}, u32[]{:S(2)}) copy-start(f32[256,256]{1,0:T(8,128)S(1)} %select_maximum_fusion.7) | copy-start | bytes 786436
  580.8 55.6 %copy-start.19 = (f32[256,64]{1,0:T(8,128)S(1)}, f32[256,64]{1,0:T(8,128)}, u32[]{:S(2)}) copy-start(f32[256,64]{1,0:T(8,128)} %gather_fusion.59) | copy-start | bytes 196612
  651.8 8.4 collective-permute-start.3
  660.9 371.3 %all-gather.19.cloned.1.call-start = ((), (), s32[]{:S(2)}) async-start(), calls=%async_computation.4 | async-start | bytes 2228224 | tf_op jit(solution)/shard_map/all_gather | solution.py:92
  707.4 171.7 %collective-permute-start.6 = (f32[64,128]{1,0:T(8,128)}, f32[64,128]{1,0:T(8,128)}, u32[]{:S(2)}, u32[]{:S(2)}) collective-permute-start(f32[64,128]{1,0:T(8,128)} %convolution_subtract_fusion.44), channel_id=1, source_target_pairs={{0,32},{32,0},{16,48},{48,16},{64,96},{96,64},{80,112},{112,80},{1... | collective-permute-start | bytes 98312 | tf_op jit(solution)/shard_map/ppermute | solution.py:14
  874.6 10.8 collective-permute-start.4
  917.1 5.8 collective-permute-start.7
  953.9 6.7 collective-permute-start.8
  991.5 9.7 collective-permute-start.9
  (261 other events, 2040.8 us)
Sparse Core Ops, SparseCore 0:
  15.2 47.5 all-gather.10
  233.7 41.2 all-gather.12
  445.4 41.2 all-gather.14
  661.0 42.0 all-gather.16
  886.2 38.5 all-gather.18
where the time goes:
time: 1210 us; the launch traced here: 1200 us
  other arithmetic  596 us (49%)
  local copies, waits for them, and re-layouts  231 us (19%)
  blocking collectives  128 us (11%)
  matrix products  110 us (9%)
  waiting for transfers between devices  81.2 us (7%)
  starting transfers between devices  34.6 us (3%)
  between operations  23.6 us (2%)
    another operation x240, other arithmetic, factor_inverse(): lower_factor = jnp.linalg.cholesky(matrix)  291 us
    another operation x160, other arithmetic, factor_inverse(): return jax.scipy.linalg.solve_triangular(lower_factor, identity, lower=True)  247 us
    all_gather x5, blocking collectives, per_device(): lax.all_gather(jnp.stack([rhs_blk, other_rhs]), 'row', axis=1, tiled=True)  128 us
    dot_general x325, matrix products, matmul_high(): return jnp.dot(left, right, precision=lax.Precision.HIGHEST)  91 us
    gather x50, local copies, waits for them, and re-layouts, spread_block(): jnp.take(jnp.take(full_matrix, jnp.maximum(src_rows, 0), axis=0), jnp.max...  60.6 us
    all_gather x5, waiting for transfers between devices, per_device(): lax.all_gather(jnp.stack([update_blk, other_upd])[:, None], ('row', 'col'...  47.1 us
    gather x30, local copies, waits for them, and re-layouts, spread_block(): jnp.take(full_matrix, jnp.maximum(src_rows, 0), axis=0)  41.8 us
    ppermute x10, starting transfers between devices, from_partner(): return lax.ppermute(block, axis, route)  34.4 us
  transfers between devices with their start and end apart: 15, of which 11 were waited for; matrix products, arithmetic and copies ran while one was open for 37% of the time, Pallas kernels for 0%

commit v1 on v0

v1 whole, which is shorter than its diff:
```python
import functools

import jax
import jax.numpy as jnp
from jax import lax
from jax.experimental import pallas as pl
from jax.experimental.pallas import tpu as pltpu
from jax.sharding import PartitionSpec as P

F32 = jnp.float32
BF16 = jnp.bfloat16
MESH = pl.DeviceIdType.MESH
LEVELS = 5
X_LEN, Z_LEN = 4, 8
S = 512
T = 128
FRONT = 2 * S
ROWS = FRONT + T
PAIRS = [(i, j) for i in range(4) for j in range(i + 1)]


def dot_nt(a, b):
    return lax.dot_general(a, b, (((1,), (1,)), ((), ())), preferred_element_type=F32)


def split(x):
    high = x.astype(BF16)
    return high, (x - high.astype(F32)).astype(BF16)


def dot3(ah, al, bh, bl):
    return dot_nt(ah, bh) + dot_nt(ah, bl) + dot_nt(al, bh)


def chol_inverse(a, store_row):
    n = a.shape[0]
    z = (
        lax.broadcasted_iota(jnp.int32, (n, n), 0) == lax.broadcasted_iota(jnp.int32, (n, n), 1)
    ).astype(F32)
    for lo in range(0, n, 8):
        m = n - lo
        cols = [jnp.broadcast_to(a[:, lo + j : lo + j + 1], (m, n)) for j in range(8)]
        top_a, top_z = a[:8], z[:8]
        more = m > 8
        if more:
            a, z = a[8:], z[8:]
        for k in range(8):
            r = lax.rsqrt(cols[k][k : k + 1])
            ck = cols[k] * r
            for j in range(k + 1, 8):
                cols[j] = cols[j] - ck * ck[j : j + 1]
            row_a = top_a[k : k + 1] * r
            row_z = top_z[k : k + 1] * r
            store_row(lo + k, row_z)
            if k < 7:
                top_a = top_a - ck[:8] * row_a
                top_z = top_z - ck[:8] * row_z
            if more:
                a = a - ck[8:] * row_a
                z = z - ck[8:] * row_z


def build_one_hot(map_row, p_ref):
    for lo in range(0, FRONT, 256):
        at = lax.broadcasted_iota(jnp.int32, (256, S), 0) + lo
        p_ref[lo : lo + 256, :] = jnp.where(at == map_row, 1.0, 0.0).astype(BF16)


def spread(item, rhs_t, p_ref, ch, cl, x_ref):
    for p, (i, j) in enumerate(PAIRS):
        block = item[p]
        h, l = split(block)
        ch[i * T : i * T + T, j * T : j * T + T] = h
        cl[i * T : i * T + T, j * T : j * T + T] = l
        if i != j:
            h, l = split(block.T)
            ch[j * T : j * T + T, i * T : i * T + T] = h
            cl[j * T : j * T + T, i * T : i * T + T] = l
    for i in range(4):
        rows = p_ref[i * 256 : i * 256 + 256, :]
        th = dot_nt(rows, ch[...]).astype(BF16)
        tl = dot_nt(rows, cl[...]).astype(BF16)
        for j in range(i + 1):
            cols = p_ref[j * 256 : j * 256 + 256, :]
            x_ref[i * 256 : i * 256 + 256, j * 256 : j * 256 + 256] = dot_nt(th, cols) + dot_nt(
                tl, cols
            )
    hh, hl = split(rhs_t[...])
    for j in range(4):
        cols = p_ref[j * 256 : j * 256 + 256, :]
        x_ref[FRONT:ROWS, j * 256 : j * 256 + 256] = dot_nt(hh, cols) + dot_nt(hl, cols)


def combine(x0, x1, coef_row, a_ref):
    for i in range(4):
        for j in range(i + 1):
            at = (slice(i * 256, i * 256 + 256), slice(j * 256, j * 256 + 256))
            total = x0[at] + x1[at]
            if i < 2:
                distance = (
                    lax.broadcasted_iota(jnp.int32, (256, 256), 0)
                    - lax.broadcasted_iota(jnp.int32, (256, 256), 1)
                    + (i - j) * 256
                )
                diag = coef_row[:, j * 256 : j * 256 + 256] + 2.0
                total = total + jnp.where(
                    distance == 0, diag, jnp.where(jnp.abs(distance) == 1, -1.0, 0.0)
                )
            a_ref[at] = total
    a_ref[FRONT:ROWS, :] = x0[FRONT:ROWS, :] + x1[FRONT:ROWS, :]


def factor(a_ref, li, vh, vl, y_t):
    def block_column(k, _):
        ks = pl.multiple_of(k * T, T)
        here = pl.ds(ks, T)

        def store_row(i, row):
            li[i : i + 1, :] = row

        chol_inverse(a_ref[here, here], store_row)
        lh, ll = split(li[...])
        for lo in range(0, ROWS, 384):
            tile = slice(lo, lo + 384)
            ah, al = split(a_ref[tile, here])
            v = dot3(ah, al, lh, ll)
            h, l = split(v)
            vh[tile, here] = h
            vl[tile, here] = l
            if lo == 768:
                y_t[:, here] = v[256:384]

        def trailing(j, _):
            there = pl.ds(pl.multiple_of(j * T, T), T)
            bh, bl = vh[there, here], vl[there, here]
            for lo in range(0, ROWS, 384):
                tile = slice(lo, lo + 384)
                a_ref[tile, there] = a_ref[tile, there] - dot3(vh[tile, here], vl[tile, here], bh, bl)
            return 0

        lax.fori_loop(k + 1, 4, trailing, 0)
        return 0

    lax.fori_loop(0, 4, block_column, 0)


def schur(a_ref, vh, vl, item, rhs_t):
    for i, j in ((0, 0), (1, 0), (1, 1)):
        ri = slice(S + i * 256, S + i * 256 + 256)
        rj = slice(S + j * 256, S + j * 256 + 256)
        c = a_ref[ri, rj] - dot3(vh[ri, :], vl[ri, :], vh[rj, :], vl[rj, :])
        for p, (bi, bj) in enumerate(PAIRS):
            if bi // 2 == i and bj // 2 == j:
                ro, co = (bi % 2) * T, (bj % 2) * T
                item[p] = c[ro : ro + T, co : co + T]
    rows = slice(FRONT, ROWS)
    for j in range(2):
        rj = slice(S + j * 256, S + j * 256 + 256)
        rhs_t[:, j * 256 : j * 256 + 256] = a_ref[rows, rj] - dot3(
            vh[rows, :], vl[rows, :], vh[rj, :], vl[rj, :]
        )


def partner_of(leaf, t):
    x, y = lax.rem(leaf, X_LEN), leaf // X_LEN
    one = jnp.int32(1)
    span_x = jnp.where(t == 0, 2 * one, jnp.where(t == 1, 4 * one, one))
    span_y = jnp.where(t == 2, 2 * one, jnp.where(t == 3, 4 * one, jnp.where(t == 4, 8 * one, one)))
    px = x - lax.rem(x, span_x) + span_x - 1 - lax.rem(x, span_x)
    py = y - lax.rem(y, span_y) + span_y - 1 - lax.rem(y, span_y)
    return py * X_LEN + px


def kernel(
    upd_ref, rhs_ref, map_ref, coef_ref,
    out_upd, out_rhs, out_sol,
    full, full_h, own, own_h, sib, sib_h, p_own, p_sib, ch, cl, x0, x1, a_ref, li, vh, vl, y_t,
    ring_send, ring_recv, core_send, core_recv,
    put_send, put_recv, fwd_send, fwd_recv, rhs_send, rhs_recv, loc,
):
    leaf = lax.axis_index("leaf")
    row = lax.axis_index("row")
    col = lax.axis_index("col")
    other = 1 - col

    up = lax.rem(row + 1, Z_LEN)
    down = lax.rem(row + Z_LEN - 1, Z_LEN)
    barrier = pltpu.get_barrier_semaphore()
    for target in ((leaf, up, col), (leaf, down, col), (leaf, row, other)):
        pl.semaphore_signal(barrier, inc=1, device_id=target, device_id_type=MESH)
    for t in range(LEVELS):
        target = (partner_of(leaf, t), row, col)
        pl.semaphore_signal(barrier, inc=1, device_id=target, device_id_type=MESH)

    here = (pl.ds(pl.multiple_of(row * 64, 64), 64), pl.ds(pl.multiple_of(col * 256, 256), 256))
    put_u = pltpu.make_async_copy(upd_ref.at[0], full.at[here], loc.at[0])
    put_h = pltpu.make_async_copy(rhs_ref.at[0], full_h.at[here[0]], loc.at[1])
    put_u.start()
    put_h.start()
    put_u.wait()
    put_h.wait()
    pl.semaphore_wait(barrier, 3 + LEVELS)

    def ring_copies(owner, to, way, step):
        rows = pl.ds(pl.multiple_of(owner * 64, 64), 64)
        cols = pl.ds(pl.multiple_of(col * 256, 256), 256)
        made = []
        for n, ref in enumerate((full.at[rows, cols], full_h.at[rows])):
            made.append(
                pltpu.make_async_remote_copy(
                    src_ref=ref, dst_ref=ref,
                    send_sem=ring_send.at[way, step, n], recv_sem=ring_recv.at[way, step, n],
                    device_id=(leaf, to, col), device_id_type=MESH,
                )
            )
        return made

    def core_copy(owner, half, n):
        rows = pl.ds(pl.multiple_of(owner * 64, 64), 64)
        ref = full.at[rows, pl.ds(pl.multiple_of(half * 256, 256), 256)]
        return pltpu.make_async_remote_copy(
            src_ref=ref, dst_ref=ref,
            send_sem=core_send.at[n], recv_sem=core_recv.at[n],
            device_id=(leaf, row, other), device_id_type=MESH,
        )

    sends = []
    owners = [row]
    for copy in ring_copies(row, up, 0, 0) + ring_copies(row, down, 1, 0):
        copy.start()
        sends.append(copy)
    crossing = [core_copy(row, col, 0)]
    crossing[0].start()
    for step in range(4):
        from_down = lax.rem(row + Z_LEN - 1 - step, Z_LEN)
        from_up = lax.rem(row + 1 + step, Z_LEN)
        for way, owner, to in ((0, from_down, up), (1, from_up, down)):
            if way == 1 and step == 3:
                continue
            for copy in ring_copies(owner, to, way, step):
                copy.wait_recv()
            if step + 1 < 4 - way:
                for copy in ring_copies(owner, to, way, step + 1):
                    copy.start()
                    sends.append(copy)
            crossing.append(core_copy(owner, col, len(crossing)))
            crossing[-1].start()
            owners.append(owner)
    for n, owner in enumerate(owners):
        core_copy(owner, other, n).wait_recv()
    for copy in sends + crossing:
        copy.wait_send()

    for p, (i, j) in enumerate(PAIRS):
        own[0, p] = full[i * T : i * T + T, j * T : j * T + T]
    for i in range(4):
        own_h[0, :, i * T : i * T + T] = full_h[i * T : i * T + T, :].T
    out_sol[0] = jnp.zeros((64, T), F32)

    def level(t, _):
        partner = partner_of(leaf, t)
        bit = lax.rem(leaf >> t, 2)
        front = 32 - (32 >> t) + (leaf >> (t + 1))

        def put(q):
            return pltpu.make_async_remote_copy(
                src_ref=own.at[t, 5 * col + q], dst_ref=sib.at[t, 5 * col + q],
                send_sem=put_send.at[q], recv_sem=put_recv.at[t, q],
                device_id=(partner, row, col), device_id_type=MESH,
            )

        def forward(q, half):
            ref = sib.at[t, 5 * half + q]
            return pltpu.make_async_remote_copy(
                src_ref=ref, dst_ref=ref,
                send_sem=fwd_send.at[q], recv_sem=fwd_recv.at[t, q],
                device_id=(leaf, row, other), device_id_type=MESH,
            )

        put_rhs = pltpu.make_async_remote_copy(
            src_ref=own_h.at[t], dst_ref=sib_h.at[t],
            send_sem=rhs_send, recv_sem=rhs_recv.at[t],
            device_id=(partner, row, col), device_id_type=MESH,
        )
        for q in range(5):
            put(q).start()
        put_rhs.start()
        build_one_hot(map_ref[pl.ds(2 * front + bit, 1), :], p_own)
        build_one_hot(map_ref[pl.ds(2 * front + 1 - bit, 1), :], p_sib)
        spread(own.at[t], own_h.at[t], p_own, ch, cl, x0)
        for q in range(5):
            put(q).wait_recv()
            forward(q, col).start()
        for q in range(5):
            forward(q, other).wait_recv()
        put_rhs.wait_recv()
        spread(sib.at[t], sib_h.at[t], p_sib, ch, cl, x1)
        for q in range(5):
            put(q).wait_send()
            forward(q, col).wait_send()
        put_rhs.wait_send()
        combine(x0, x1, coef_ref[pl.ds(front, 1), :], a_ref)
        factor(a_ref, li, vh, vl, y_t)
        schur(a_ref, vh, vl, own.at[t + 1], own_h.at[t + 1])

        low = lax.rem(leaf, 2 << t)
        keep = (low == (1 << t)) | ((t == LEVELS - 1) & (lax.rem(leaf, 1 << t) == 0))

        @pl.when(keep)
        def _():
            block = y_t[:, pl.ds(pl.multiple_of(row // 2 * T, T), T)].T
            li[...] = block
            out_sol[0] = li[pl.ds(pl.multiple_of(lax.rem(row, 2) * 64, 64), 64), :]

        return 0

    lax.fori_loop(0, LEVELS, level, 0)

    for p, (i, j) in enumerate(PAIRS):
        block = own[LEVELS, p]
        full[i * T : i * T + T, j * T : j * T + T] = block
        if i != j:
            full[j * T : j * T + T, i * T : i * T + T] = block.T
    for i in range(4):
        full_h[i * T : i * T + T, :] = own_h[LEVELS, :, i * T : i * T + T].T
    out_upd[...] = full[here]
    out_rhs[...] = full_h[here[0], :]


def per_device(leaf_update, leaf_rhs, child_rows, separator_coef):
    vmem = pl.BlockSpec(memory_space=pltpu.VMEM)
    dma = pltpu.SemaphoreType.DMA
    return pl.pallas_call(
        kernel,
        name="multifrontal",
        out_shape=(
            jax.ShapeDtypeStruct((64, 256), F32),
            jax.ShapeDtypeStruct((64, T), F32),
            jax.ShapeDtypeStruct((1, 64, T), F32),
        ),
        in_specs=[vmem] * 4,
        out_specs=(vmem,) * 3,
        scratch_shapes=[
            pltpu.VMEM((S, S), F32),
            pltpu.VMEM((S, T), F32),
            pltpu.VMEM((LEVELS + 1, 10, T, T), F32),
            pltpu.VMEM((LEVELS + 1, T, S), F32),
            pltpu.VMEM((LEVELS, 10, T, T), F32),
            pltpu.VMEM((LEVELS, T, S), F32),
            pltpu.VMEM((FRONT, S), BF16),
            pltpu.VMEM((FRONT, S), BF16),
            pltpu.VMEM((S, S), BF16),
            pltpu.VMEM((S, S), BF16),
            pltpu.VMEM((ROWS, FRONT), F32),
            pltpu.VMEM((ROWS, FRONT), F32),
            pltpu.VMEM((ROWS, FRONT), F32),
            pltpu.VMEM((T, T), F32),
            pltpu.VMEM((ROWS, S), BF16),
            pltpu.VMEM((ROWS, S), BF16),
            pltpu.VMEM((T, S), F32),
            dma((2, 4, 2)),
            dma((2, 4, 2)),
            dma((8,)),
            dma((8,)),
            dma((5,)),
            dma((LEVELS, 5)),
            dma((5,)),
            dma((LEVELS, 5)),
            dma,
            dma((LEVELS,)),
            dma((2,)),
        ],
        compiler_params=pltpu.CompilerParams(
            collective_id=0, has_side_effects=True, vmem_limit_bytes=56 * 1024 * 1024
        ),
    )(leaf_update, leaf_rhs, child_rows.reshape(-1, S), separator_coef)


def solution(mesh):
    in_specs = (P("leaf", "row", "col"), P("leaf", "row", "col"), P(), P())
    out_specs = (P("row", "col"), P("row", "col"), P("leaf", "row", "col"))
    return jax.shard_map(
        per_device, mesh=mesh, in_specs=in_specs, out_specs=out_specs, check_vma=False
    )
```

time: 1210 us -> 250 us (0.21)
  the two profiles are of different devices: /device:TPU:24 before, /device:TPU:72 now
where the time goes in v1:
time: 250 us
  Pallas kernels  244 us (98%)
  local copies, waits for them, and re-layouts  4.5 us (2%)
    pallas_call x1, Pallas kernels, per_device(): pl.pallas_call(kernel, name='multifrontal', out_shape=(jax.ShapeDtypeStru...  244 us

profile of v1, /device:TPU:72, one launch (start us, length us, event | category | flops | bytes accessed | tf_op | source)
XLA Modules:
  0.0 249.6 jit_solution(7746944970632047299)
XLA Ops:
  0.6 1.6 reshape.9.map_ref
  2.3 244.5 %multifrontal.1 = (f32[64,256]{1,0:T(8,128)}, f32[64,128]{1,0:T(8,128)}, f32[1,64,128]{2,1,0:T(8,128)}) custom-call(f32[1,64,256]{2,1,0:T(8,128)} %upd_ref.1, f32[1,64,128]{2,1,0:T(8,128)} %rhs_ref.1, s32[62,512]{1,0:T(8,128)} %reshape.9.map_ref, f32[31,512]{1,0:T(8,128)} %coef_ref.1), custom_call_target="tpu_custom_call" | custom-call | tf_op jit(solution)/shard_map/multifrontal/pallas_call | solution.py:333
  246.8 0.0 copy-start.1
  246.8 1.5 copy.10
  248.2 0.0 copy-done.1
  248.2 0.0 copy-start
  248.2 0.6 copy.11
  248.9 0.2 copy-done
  249.0 0.6 copy.12
Async XLA Ops:
  246.8 1.5 copy-start.1
  248.2 0.8 copy-start

commit v2 on v1

v2 whole, which is shorter than its diff:
```python
import functools

import jax
import jax.numpy as jnp
from jax import lax
from jax.experimental import pallas as pl
from jax.experimental.pallas import tpu as pltpu
from jax.sharding import PartitionSpec as P

F32 = jnp.float32
BF16 = jnp.bfloat16
MESH = pl.DeviceIdType.MESH
LEVELS = 5
X_LEN, Z_LEN = 4, 8
S = 512
T = 128
FRONT = 2 * S
ROWS = FRONT + 16
PAIRS = [(i, j) for i in range(4) for j in range(i + 1)]


def dot_nt(a, b):
    return lax.dot_general(a, b, (((1,), (1,)), ((), ())), preferred_element_type=F32)


def split(x):
    high = x.astype(BF16)
    return high, (x - high.astype(F32)).astype(BF16)


def dot_tn(a, b):
    return lax.dot_general(a, b, (((0,), (0,)), ((), ())), preferred_element_type=F32)


def dot3(ah, al, bh, bl):
    return dot_nt(ah, bh) + dot_nt(ah, bl) + dot_nt(al, bh)


def eliminate(a, base, store_row):
    m, n = a.shape
    lane = lax.broadcasted_iota(jnp.int32, (8, n), 1)
    sub = lax.broadcasted_iota(jnp.int32, (8, n), 0)

    def spread_col(rows, at):
        return jnp.broadcast_to(rows[:, at : at + 1], rows.shape)

    top = [spread_col(a[:8], base + j) for j in range(8)]
    for lo in range(0, m, 8):
        at = base + lo
        inside = (lane >= at) & (lane < at + 8)
        head = jnp.where(inside, jnp.where(lane - at == sub, 1.0, 0.0), a[:8])
        left = m - lo - 8
        if left:
            low = [spread_col(a[8:], at + j) for j in range(8)]
            ahead = [spread_col(a[8:16], at + 8 + j) for j in range(8)]
            a = jnp.concatenate(
                [jnp.where(inside, 0.0, a[i : i + 8]) for i in range(8, left + 8, 8)], axis=0
            )
        for k in range(8):
            pivot = top[k][k : k + 1]
            inverse = 1.0 / pivot
            row = head[k : k + 1]
            store_row(lo + k, row * lax.rsqrt(pivot))
            if left:
                below = low[k] * inverse
            for j in range(k + 1, 8):
                factor_row = top[k][j : j + 1]
                top[j] = top[j] - (top[k] * factor_row) * inverse
                if left:
                    low[j] = low[j] - below * factor_row
            if left:
                for j in range(8):
                    ahead[j] = ahead[j] - below[:8] * low[k][j : j + 1]
                a = a - below * row
            if k < 7:
                head = head - (top[k] * inverse) * row
        if left:
            top = ahead


def build_one_hot(map_row, p_ref):
    for lo in range(0, FRONT, 256):
        at = lax.broadcasted_iota(jnp.int32, (256, S), 0) + lo
        p_ref[lo : lo + 256, :] = jnp.where(at == map_row, 1.0, 0.0).astype(BF16)


def expand(item, ch, cl):
    for p, (i, j) in enumerate(PAIRS):
        block = jnp.concatenate([item[2 * p], item[2 * p + 1]], axis=0)
        h, l = split(block)
        ch[i * T : i * T + T, j * T : j * T + T] = h
        cl[i * T : i * T + T, j * T : j * T + T] = l
        if i != j:
            h, l = split(block.T)
            ch[j * T : j * T + T, i * T : i * T + T] = h
            cl[j * T : j * T + T, i * T : i * T + T] = l


def spread_rows(i, p_ref, ch, cl, th, tl):
    tile = slice(i * 256, i * 256 + 256)
    rows = p_ref[tile, :]
    th[tile, :] = dot_nt(rows, ch[...]).astype(BF16)
    tl[tile, :] = dot_nt(rows, cl[...]).astype(BF16)


def spread_cols(i, p_ref, th, tl, x_ref):
    tile = slice(i * 256, i * 256 + 256)
    for j in range(i + 1):
        cols = p_ref[j * 256 : j * 256 + 256, :]
        x_ref[tile, j * 256 : j * 256 + 256] = dot_nt(th[tile, :], cols) + dot_nt(tl[tile, :], cols)


def spread_rhs(rhs_t, p_ref, x_ref):
    both = jnp.concatenate(split(rhs_t[...]), axis=0)
    for j in range(4):
        x = dot_nt(both, p_ref[j * 256 : j * 256 + 256, :])
        x_ref[FRONT:ROWS, j * 256 : j * 256 + 256] = x[:16] + x[16:]


def combine(x0, x1, coef_row, a_ref):
    for i in range(4):
        for j in range(i + 1):
            at = (slice(i * 256, i * 256 + 256), slice(j * 256, j * 256 + 256))
            total = x0[at] + x1[at]
            if i < 2:
                distance = (
                    lax.broadcasted_iota(jnp.int32, (256, 256), 0)
                    - lax.broadcasted_iota(jnp.int32, (256, 256), 1)
                    + (i - j) * 256
                )
                diag = coef_row[:, j * 256 : j * 256 + 256] + 2.0
                total = total + jnp.where(
                    distance == 0, diag, jnp.where(jnp.abs(distance) == 1, -1.0, 0.0)
                )
            a_ref[at] = total
    a_ref[FRONT:ROWS, :] = x0[FRONT:ROWS, :] + x1[FRONT:ROWS, :]


def factor(a_ref, li, raw, diag, vh, vl, y_t):
    vh[...] = jnp.zeros_like(vh)
    vl[...] = jnp.zeros_like(vl)
    li[...] = jnp.zeros_like(li)
    diag[...] = a_ref[0:T, 0:T]
    tiles = [slice(0, 256), slice(256, 512), slice(512, 768), slice(768, ROWS)]

    def panel(k):
        here = pl.ds(pl.multiple_of(k * T, T), T)
        lh, ll = split(li[...])
        for tile in tiles:
            ah, al = split(a_ref[tile, here])
            v = dot3(ah, al, lh, ll)
            h, l = split(v)
            vh[tile, here] = h
            vl[tile, here] = l
            if tile.stop == ROWS:
                y_t[:, here] = v[256:]

    def block_column(k, _):
        here = pl.ds(pl.multiple_of(k * T, T), T)
        after = pl.ds(pl.multiple_of(k * T + T, T), T)
        block = diag[...]

        def store_upper(i, row):
            raw[i : i + 1, :] = row

        def store_lower(i, row):
            raw[64 + i : 65 + i, :] = row

        eliminate(block[:64], 0, store_upper)
        panel(jnp.maximum(k - 1, 0))
        lanes = lax.broadcasted_iota(jnp.int32, (64, T), 1)
        valid = (lanes <= lax.broadcasted_iota(jnp.int32, (64, T), 0)) | (lanes >= 64)
        rh, rl = split(jnp.where(valid, raw[0:64, :], 0.0))
        lower = jnp.where(lanes < 64, 0.0, block[64:])
        lower = lower - (dot_tn(rh, rh) + dot_tn(rh, rl) + dot_tn(rl, rh))[64:]
        eliminate(lower, 64, store_lower)
        bh, bl = vh[here, :], vl[here, :]
        for tile in tiles:
            a_ref[tile, here] = a_ref[tile, here] - dot3(vh[tile, :], vl[tile, :], bh, bl)
        nh, nl = vh[after, :], vl[after, :]
        next_block = a_ref[after, after] - dot3(nh, nl, nh, nl)
        at = lax.broadcasted_iota(jnp.int32, (T, T), 0)
        inverse = jnp.where(lax.broadcasted_iota(jnp.int32, (T, T), 1) <= at, raw[...], 0.0)
        li[...] = inverse
        lh, ll = split(inverse)
        ah, al = split(a_ref[after, here])
        h, l = split(dot3(ah, al, lh, ll))
        diag[...] = next_block - dot3(h, l, h, l)
        vh[after, here] = h
        vl[after, here] = l
        return 0

    lax.fori_loop(0, 4, block_column, 0)
    panel(3)


def schur(a_ref, vh, vl, item):
    for i, j in ((0, 0), (1, 0), (1, 1)):
        ri = slice(S + i * 256, S + i * 256 + 256)
        rj = slice(S + j * 256, S + j * 256 + 256)
        c = a_ref[ri, rj] - dot3(vh[ri, :], vl[ri, :], vh[rj, :], vl[rj, :])
        for p, (bi, bj) in enumerate(PAIRS):
            if bi // 2 == i and bj // 2 == j:
                ro, co = (bi % 2) * T, (bj % 2) * T
                item[2 * p] = c[ro : ro + 64, co : co + T]
                item[2 * p + 1] = c[ro + 64 : ro + T, co : co + T]


def schur_rhs(a_ref, vh, vl, rhs_t):
    rows = slice(FRONT, ROWS)
    for j in range(2):
        rj = slice(S + j * 256, S + j * 256 + 256)
        rhs_t[:, j * 256 : j * 256 + 256] = a_ref[rows, rj] - dot3(
            vh[rows, :], vl[rows, :], vh[rj, :], vl[rj, :]
        )


def partner_of(leaf, t):
    x, y = lax.rem(leaf, X_LEN), leaf // X_LEN
    one = jnp.int32(1)
    span_x = jnp.where(t == 0, 2 * one, jnp.where(t == 1, 4 * one, one))
    span_y = jnp.where(t == 2, 2 * one, jnp.where(t == 3, 4 * one, jnp.where(t == 4, 8 * one, one)))
    px = x - lax.rem(x, span_x) + span_x - 1 - lax.rem(x, span_x)
    py = y - lax.rem(y, span_y) + span_y - 1 - lax.rem(y, span_y)
    return py * X_LEN + px


def kernel(
    upd_ref, rhs_ref, map_ref, coef_ref,
    out_upd, out_rhs, out_sol,
    full, slab_out, slab_in, last_out, last_in,
    own, own_h, sib, sib_h, p_own, p_sib, ch, cl, th, tl, x0, x1, a_ref, li, raw, diag, vh, vl, y_t, y_kept,
    ring_send, ring_recv, core_send, core_recv, slab_send, slab_recv, last_send, last_recv,
    put_send, put_recv, row_send, row_recv, near_send, near_recv, far_send, far_recv,
    rhs_send, rhs_recv, loc,
):
    leaf = lax.axis_index("leaf")
    row = lax.axis_index("row")
    col = lax.axis_index("col")
    other = 1 - col
    beside = row + 1 - 2 * lax.rem(row, 2)
    quarter = 2 * lax.rem(row, 2) + col
    quarter_row = 2 * lax.rem(beside, 2) + col

    def to_peer(src, dst, send_sem, recv_sem, device):
        return pltpu.make_async_remote_copy(
            src_ref=src, dst_ref=dst, send_sem=send_sem, recv_sem=recv_sem,
            device_id=device, device_id_type=MESH,
        )

    barrier = pltpu.get_barrier_semaphore()
    peers = [lax.rem(row + d, Z_LEN) for d in range(Z_LEN)]
    targets = [(leaf, peers[d], col) for d in range(1, Z_LEN)] + [(leaf, row, other)]
    targets += [(partner_of(leaf, t), row, col) for t in range(LEVELS)]
    for target in targets:
        pl.semaphore_signal(barrier, inc=1, device_id=target, device_id_type=MESH)

    here = (pl.ds(pl.multiple_of(row * 64, 64), 64), pl.ds(pl.multiple_of(col * 256, 256), 256))
    put_own = pltpu.make_async_copy(upd_ref.at[0], full.at[here], loc)
    put_own.start()
    slabs = rhs_ref[0].T
    for r in range(Z_LEN):
        slab_out[r, :, 0:64] = slabs[r * 16 : r * 16 + 16, :]
    put_own.wait()
    pl.semaphore_wait(barrier, len(targets))

    up, down = peers[1], peers[Z_LEN - 1]

    def ring_copy(owner, to, way, step):
        rows = pl.ds(pl.multiple_of(owner * 64, 64), 64)
        ref = full.at[rows, here[1]]
        return to_peer(
            ref, ref, ring_send.at[way, step], ring_recv.at[way, step], (leaf, to, col)
        )

    def core_copy(owner, half, n):
        rows = pl.ds(pl.multiple_of(owner * 64, 64), 64)
        ref = full.at[rows, pl.ds(pl.multiple_of(half * 256, 256), 256)]
        return to_peer(ref, ref, core_send.at[n], core_recv.at[n], (leaf, row, other))

    sends = [ring_copy(row, up, 0, 0), ring_copy(row, down, 1, 0), core_copy(row, col, 0)]
    for copy in sends:
        copy.start()
    slab_copies = [
        to_peer(
            slab_out.at[peers[d]], slab_in.at[row], slab_send.at[d], slab_recv.at[d],
            (leaf, peers[d], col),
        )
        for d in range(1, Z_LEN)
    ]
    for copy in slab_copies:
        copy.start()
    slab_in[row] = slab_out[row]
    owners = [row]
    for step in range(4):
        for way, owner, to in ((0, peers[7 - step], up), (1, peers[1 + step], down)):
            if way == 1 and step == 3:
                continue
            ring_copy(owner, to, way, step).wait_recv()
            if step + 1 < 4 - way:
                sends.append(ring_copy(owner, to, way, step + 1))
                sends[-1].start()
            sends.append(core_copy(owner, col, len(owners)))
            sends[-1].start()
            owners.append(owner)
    for n, owner in enumerate(owners):
        core_copy(owner, other, n).wait_recv()
    for copy in sends:
        copy.wait_send()
    for copy in slab_copies:
        copy.wait()

    def puts(t):
        partner = partner_of(leaf, t)
        return [
            to_peer(
                own.at[t, 5 * quarter + q], sib.at[t, 5 * quarter + q],
                put_send.at[q], put_recv.at[t, q], (partner, row, col),
            )
            for q in range(5)
        ]

    def put_rhs(t):
        return to_peer(
            own_h.at[t], sib_h.at[t], rhs_send, rhs_recv.at[t], (partner_of(leaf, t), row, col)
        )

    for p, (i, j) in enumerate(PAIRS):
        for half in range(2):
            lo = i * T + half * 64
            own[0, 2 * p + half] = full[lo : lo + 64, j * T : j * T + T]
    for copy in puts(0):
        copy.start()
    for i in range(4):
        own_h[0, :, i * T : i * T + T] = jnp.concatenate(
            [slab_in[2 * i, :, 0:64], slab_in[2 * i + 1, :, 0:64]], axis=1
        )
    put_rhs(0).start()

    def level(t, _):
        bit = lax.rem(leaf >> t, 2)
        front = 32 - (32 >> t) + (leaf >> (t + 1))

        def share(part, q, send, recv, device):
            ref = sib.at[t, 5 * part + q]
            return to_peer(ref, ref, send.at[q], recv.at[t, q], device)

        over_core, over_row = (leaf, row, other), (leaf, beside, col)
        arrive = puts(t)
        to_near = [share(quarter, q, near_send, near_recv, over_core) for q in range(5)]
        to_row = [share(quarter, q, row_send, row_recv, over_row) for q in range(5)]
        to_far = [share(quarter_row, q, far_send, far_recv, over_core) for q in range(5)]

        def pass_on(q):
            arrive[q].wait_recv()
            to_row[q].start()
            to_near[q].start()

        def pass_far(q):
            to_row[q].wait_recv()
            to_far[q].start()

        build_one_hot(map_ref[front, pl.ds(bit, 1), :], p_own)
        expand(own.at[t], ch, cl)
        spread_rows(0, p_own, ch, cl, th, tl)
        spread_cols(0, p_own, th, tl, x0)
        pass_on(0)
        spread_rows(1, p_own, ch, cl, th, tl)
        pass_on(1)
        spread_cols(1, p_own, th, tl, x0)
        pass_on(2)
        spread_rows(2, p_own, ch, cl, th, tl)
        pass_on(3)
        pass_far(0)
        spread_cols(2, p_own, th, tl, x0)
        pass_on(4)
        pass_far(1)
        spread_rows(3, p_own, ch, cl, th, tl)
        pass_far(2)
        spread_cols(3, p_own, th, tl, x0)
        pass_far(3)
        build_one_hot(map_ref[front, pl.ds(1 - bit, 1), :], p_sib)
        pass_far(4)
        spread_rhs(own_h.at[t], p_own, x0)
        put_rhs(t).wait()
        spread_rhs(sib_h.at[t], p_sib, x1)
        for q in range(5):
            to_near[q].wait_recv()
            to_far[q].wait_recv()
        expand(sib.at[t], ch, cl)
        for i in range(4):
            spread_rows(i, p_sib, ch, cl, th, tl)
            spread_cols(i, p_sib, th, tl, x1)
        for q in range(5):
            for copy in (arrive[q], to_near[q], to_row[q], to_far[q]):
                copy.wait_send()
        combine(x0, x1, coef_ref[pl.ds(front, 1), :], a_ref)
        factor(a_ref, li, raw, diag, vh, vl, y_t)
        schur(a_ref, vh, vl, own.at[t + 1])

        @pl.when(t < LEVELS - 1)
        def _():
            for copy in puts(t + 1):
                copy.start()

        schur_rhs(a_ref, vh, vl, own_h.at[t + 1])

        @pl.when(t < LEVELS - 1)
        def _():
            put_rhs(t + 1).start()

        low = lax.rem(leaf, 2 << t)
        keep = (low == (1 << t)) | ((t == LEVELS - 1) & (lax.rem(leaf, 1 << t) == 0))

        @pl.when(keep)
        def _():
            y_kept[...] = y_t[...]

        return 0

    lax.fori_loop(0, LEVELS, level, 0)

    for r in range(Z_LEN):
        last_out[r, 0:16, 0:64] = own_h[LEVELS, :, r * 64 : r * 64 + 64]
        last_out[r, 16:32, 0:64] = y_kept[:, r * 64 : r * 64 + 64]
    last_copies = [
        to_peer(
            last_out.at[peers[d]], last_in.at[row], last_send.at[d], last_recv.at[d],
            (leaf, peers[d], col),
        )
        for d in range(1, Z_LEN)
    ]
    for copy in last_copies:
        copy.start()
    last_in[row] = last_out[row]
    for p, (i, j) in enumerate(PAIRS):
        block = jnp.concatenate([own[LEVELS, 2 * p], own[LEVELS, 2 * p + 1]], axis=0)
        full[i * T : i * T + T, j * T : j * T + T] = block
        if i != j:
            full[j * T : j * T + T, i * T : i * T + T] = block.T
    out_upd[...] = full[here]
    for copy in last_copies:
        copy.wait()
    out_rhs[...] = jnp.concatenate([last_in[r, 0:16, 0:64] for r in range(Z_LEN)], axis=0).T
    out_sol[0] = jnp.concatenate([last_in[r, 16:32, 0:64] for r in range(Z_LEN)], axis=0).T


def per_device(leaf_update, leaf_rhs, child_rows, separator_coef):
    vmem = pl.BlockSpec(memory_space=pltpu.VMEM)
    dma = pltpu.SemaphoreType.DMA
    return pl.pallas_call(
        kernel,
        name="multifrontal",
        out_shape=(
            jax.ShapeDtypeStruct((64, 256), F32),
            jax.ShapeDtypeStruct((64, T), F32),
            jax.ShapeDtypeStruct((1, 64, T), F32),
        ),
        in_specs=[vmem] * 4,
        out_specs=(vmem,) * 3,
        scratch_shapes=[
            pltpu.VMEM((S, S), F32),
            pltpu.VMEM((Z_LEN, 16, T), F32),
            pltpu.VMEM((Z_LEN, 16, T), F32),
            pltpu.VMEM((Z_LEN, 32, T), F32),
            pltpu.VMEM((Z_LEN, 32, T), F32),
            pltpu.VMEM((LEVELS + 1, 20, 64, T), F32),
            pltpu.VMEM((LEVELS + 1, 16, S), F32),
            pltpu.VMEM((LEVELS, 20, 64, T), F32),
            pltpu.VMEM((LEVELS, 16, S), F32),
            pltpu.VMEM((FRONT, S), BF16),
            pltpu.VMEM((FRONT, S), BF16),
            pltpu.VMEM((S, S), BF16),
            pltpu.VMEM((S, S), BF16),
            pltpu.VMEM((FRONT, S), BF16),
            pltpu.VMEM((FRONT, S), BF16),
            pltpu.VMEM((ROWS, FRONT), F32),
            pltpu.VMEM((ROWS, FRONT), F32),
            pltpu.VMEM((ROWS, FRONT), F32),
            pltpu.VMEM((T, T), F32),
            pltpu.VMEM((T, T), F32),
            pltpu.VMEM((T, T), F32),
            pltpu.VMEM((ROWS, S), BF16),
            pltpu.VMEM((ROWS, S), BF16),
            pltpu.VMEM((16, S), F32),
            pltpu.VMEM((16, S), F32),
            dma((2, 4)), dma((2, 4)),
            dma((8,)), dma((8,)),
            dma((8,)), dma((8,)),
            dma((8,)), dma((8,)),
            dma((5,)), dma((LEVELS, 5)),
            dma((5,)), dma((LEVELS, 5)),
            dma((5,)), dma((LEVELS, 5)),
            dma((5,)), dma((LEVELS, 5)),
            dma, dma((LEVELS,)),
            dma,
        ],
        compiler_params=pltpu.CompilerParams(
            collective_id=0, has_side_effects=True, vmem_limit_bytes=56 * 1024 * 1024
        ),
    )(leaf_update, leaf_rhs, child_rows, separator_coef)


def solution(mesh):
    in_specs = (P("leaf", "row", "col"), P("leaf", "row", "col"), P(), P())
    out_specs = (P("row", "col"), P("row", "col"), P("leaf", "row", "col"))
    return jax.shard_map(
        per_device, mesh=mesh, in_specs=in_specs, out_specs=out_specs, check_vma=False
    )
```

time: 250 us -> 188 us (0.75)
  the two profiles are of different devices: /device:TPU:72 before, /device:TPU:1 now
where the time goes in v2:
time: 188 us; the launch traced here: 185 us
  Pallas kernels  181 us (96%)
  local copies, waits for them, and re-layouts  2.87 us (2%)
    pallas_call x1, Pallas kernels, per_device(): pl.pallas_call(kernel, name='multifrontal', out_shape=(jax.ShapeDtypeStru...  181 us

profile of v2, /device:TPU:1, one launch (start us, length us, event | category | flops | bytes accessed | tf_op | source)
XLA Modules:
  0.0 184.7 jit_solution(5596805903408434918)
XLA Ops:
  0.6 181.2 %multifrontal.1 = (f32[64,256]{1,0:T(8,128)}, f32[64,128]{1,0:T(8,128)}, f32[1,64,128]{2,1,0:T(8,128)}) custom-call(f32[1,64,256]{2,1,0:T(8,128)} %upd_ref.1, f32[1,64,128]{2,1,0:T(8,128)} %rhs_ref.1, s32[31,2,512]{2,1,0:T(2,128)} %map_ref.1, f32[31,512]{1,0:T(8,128)} %coef_ref.1), custom_call_target="tpu_custom_call" | custom-call | tf_op jit(solution)/shard_map/multifrontal/pallas_call | solution.py:451
  181.8 0.0 copy-start.1
  181.8 1.5 copy.10
  183.3 0.0 copy-done.1
  183.3 0.0 copy-start
  183.3 0.6 copy.11
  183.9 0.2 copy-done
  184.1 0.6 copy.12
Async XLA Ops:
  181.8 1.5 copy-start.1
  183.3 0.8 copy-start

commit v3 on v2

--- a/solution.py
+++ b/solution.py
@@ -103,9 +103,9 @@
     tl[tile, :] = dot_nt(rows, cl[...]).astype(BF16)
 
 
-def spread_cols(i, p_ref, th, tl, x_ref):
+def spread_cols(i, p_ref, th, tl, x_ref, first=0):
     tile = slice(i * 256, i * 256 + 256)
-    for j in range(i + 1):
+    for j in range(first, i + 1):
         cols = p_ref[j * 256 : j * 256 + 256, :]
         x_ref[tile, j * 256 : j * 256 + 256] = dot_nt(th[tile, :], cols) + dot_nt(tl[tile, :], cols)
 
@@ -118,28 +118,29 @@
 
 
 def combine(x0, x1, coef_row, a_ref):
-    for i in range(4):
-        for j in range(i + 1):
-            at = (slice(i * 256, i * 256 + 256), slice(j * 256, j * 256 + 256))
-            total = x0[at] + x1[at]
-            if i < 2:
-                distance = (
-                    lax.broadcasted_iota(jnp.int32, (256, 256), 0)
-                    - lax.broadcasted_iota(jnp.int32, (256, 256), 1)
-                    + (i - j) * 256
-                )
-                diag = coef_row[:, j * 256 : j * 256 + 256] + 2.0
-                total = total + jnp.where(
-                    distance == 0, diag, jnp.where(jnp.abs(distance) == 1, -1.0, 0.0)
-                )
-            a_ref[at] = total
+    for i, j in ((0, 0), (1, 0), (1, 1)):
+        at = (slice(i * 256, i * 256 + 256), slice(j * 256, j * 256 + 256))
+        distance = (
+            lax.broadcasted_iota(jnp.int32, (256, 256), 0)
+            - lax.broadcasted_iota(jnp.int32, (256, 256), 1)
+            + (i - j) * 256
+        )
+        diag = coef_row[:, j * 256 : j * 256 + 256] + 2.0
+        stencil = jnp.where(distance == 0, diag, jnp.where(jnp.abs(distance) == 1, -1.0, 0.0))
+        a_ref[at] = x0[at] + x1[at] + stencil
+    for i, j in ((2, 2), (3, 2), (3, 3)):
+        at = (slice(i * 256, i * 256 + 256), slice(j * 256, j * 256 + 256))
+        a_ref[at] = x0[at] + x1[at]
     a_ref[FRONT:ROWS, :] = x0[FRONT:ROWS, :] + x1[FRONT:ROWS, :]
 
 
-def factor(a_ref, li, raw, diag, vh, vl, y_t):
+def clear(li, vh, vl):
     vh[...] = jnp.zeros_like(vh)
     vl[...] = jnp.zeros_like(vl)
     li[...] = jnp.zeros_like(li)
+
+
+def factor(a_ref, x0, x1, p_sib, th, tl, li, raw, diag, vh, vl, y_t):
     diag[...] = a_ref[0:T, 0:T]
     tiles = [slice(0, 256), slice(256, 512), slice(512, 768), slice(768, ROWS)]
 
@@ -168,6 +169,9 @@
 
         eliminate(block[:64], 0, store_upper)
         panel(jnp.maximum(k - 1, 0))
+        for tile in (slice(512, 768), slice(768, FRONT)):
+            x1[tile, here] = dot_nt(th[tile, :], p_sib[here, :]) + dot_nt(tl[tile, :], p_sib[here, :])
+            a_ref[tile, here] = x0[tile, here] + x1[tile, here]
         lanes = lax.broadcasted_iota(jnp.int32, (64, T), 1)
         valid = (lanes <= lax.broadcasted_iota(jnp.int32, (64, T), 0)) | (lanes >= 64)
         rh, rl = split(jnp.where(valid, raw[0:64, :], 0.0))
@@ -250,7 +254,7 @@
 
     barrier = pltpu.get_barrier_semaphore()
     peers = [lax.rem(row + d, Z_LEN) for d in range(Z_LEN)]
-    targets = [(leaf, peers[d], col) for d in range(1, Z_LEN)] + [(leaf, row, other)]
+    targets = [(leaf, peers[d], col) for d in range(1, Z_LEN)] + [(leaf, row, other), (leaf, beside, other)]
     targets += [(partner_of(leaf, t), row, col) for t in range(LEVELS)]
     for target in targets:
         pl.semaphore_signal(barrier, inc=1, device_id=target, device_id_type=MESH)
@@ -349,16 +353,20 @@
         arrive = puts(t)
         to_near = [share(quarter, q, near_send, near_recv, over_core) for q in range(5)]
         to_row = [share(quarter, q, row_send, row_recv, over_row) for q in range(5)]
-        to_far = [share(quarter_row, q, far_send, far_recv, over_core) for q in range(5)]
+        to_far = [share(quarter_row, q, far_send, far_recv, over_core) for q in range(4)]
+        to_far.append(share(quarter, 4, far_send, far_recv, (leaf, beside, other)))
 
         def pass_on(q):
             arrive[q].wait_recv()
             to_row[q].start()
+            if q == 4:
+                to_far[q].start()
             to_near[q].start()
 
         def pass_far(q):
             to_row[q].wait_recv()
-            to_far[q].start()
+            if q < 4:
+                to_far[q].start()
 
         build_one_hot(map_ref[front, pl.ds(bit, 1), :], p_own)
         expand(own.at[t], ch, cl)
@@ -382,6 +390,7 @@
         build_one_hot(map_ref[front, pl.ds(1 - bit, 1), :], p_sib)
         pass_far(4)
         spread_rhs(own_h.at[t], p_own, x0)
+        clear(li, vh, vl)
         put_rhs(t).wait()
         spread_rhs(sib_h.at[t], p_sib, x1)
         for q in range(5):
@@ -390,23 +399,20 @@
         expand(sib.at[t], ch, cl)
         for i in range(4):
             spread_rows(i, p_sib, ch, cl, th, tl)
-            spread_cols(i, p_sib, th, tl, x1)
+        for i in range(4):
+            spread_cols(i, p_sib, th, tl, x1, first=0 if i < 2 else 2)
         for q in range(5):
             for copy in (arrive[q], to_near[q], to_row[q], to_far[q]):
                 copy.wait_send()
         combine(x0, x1, coef_ref[pl.ds(front, 1), :], a_ref)
-        factor(a_ref, li, raw, diag, vh, vl, y_t)
-        schur(a_ref, vh, vl, own.at[t + 1])
+        factor(a_ref, x0, x1, p_sib, th, tl, li, raw, diag, vh, vl, y_t)
 
         @pl.when(t < LEVELS - 1)
         def _():
+            schur(a_ref, vh, vl, own.at[t + 1])
             for copy in puts(t + 1):
                 copy.start()
-
-        schur_rhs(a_ref, vh, vl, own_h.at[t + 1])
-
-        @pl.when(t < LEVELS - 1)
-        def _():
+            schur_rhs(a_ref, vh, vl, own_h.at[t + 1])
             put_rhs(t + 1).start()
 
         low = lax.rem(leaf, 2 << t)
@@ -420,6 +426,7 @@
 
     lax.fori_loop(0, LEVELS, level, 0)
 
+    schur_rhs(a_ref, vh, vl, own_h.at[LEVELS])
     for r in range(Z_LEN):
         last_out[r, 0:16, 0:64] = own_h[LEVELS, :, r * 64 : r * 64 + 64]
         last_out[r, 16:32, 0:64] = y_kept[:, r * 64 : r * 64 + 64]
@@ -433,6 +440,7 @@
     for copy in last_copies:
         copy.start()
     last_in[row] = last_out[row]
+    schur(a_ref, vh, vl, own.at[LEVELS])
     for p, (i, j) in enumerate(PAIRS):
         block = jnp.concatenate([own[LEVELS, 2 * p], own[LEVELS, 2 * p + 1]], axis=0)
         full[i * T : i * T + T, j * T : j * T + T] = block

time: 188 us -> 183 us (0.973); the launches traced: 185 us -> 182 us
  Pallas kernels: 181 us -> 179 us
    pallas_call x1, Pallas kernels: 181 us -> 179 us  [per_device(): pl.pallas_call(kernel, name='multifrontal', out_shape=(jax.ShapeDtypeStru...]
where the time goes in v3:
time: 183 us; the launch traced here: 182 us
  Pallas kernels  179 us (98%)
  local copies, waits for them, and re-layouts  2.87 us (2%)
    pallas_call x1, Pallas kernels, per_device(): pl.pallas_call(kernel, name='multifrontal', out_shape=(jax.ShapeDtypeStru...  179 us

profile of v3, /device:TPU:1, one launch (start us, length us, event | category | flops | bytes accessed | tf_op | source)
XLA Modules:
  0.0 182.5 jit_solution(2299373188191055799)
XLA Ops:
  0.6 178.9 %multifrontal.1 = (f32[64,256]{1,0:T(8,128)}, f32[64,128]{1,0:T(8,128)}, f32[1,64,128]{2,1,0:T(8,128)}) custom-call(f32[1,64,256]{2,1,0:T(8,128)} %upd_ref.1, f32[1,64,128]{2,1,0:T(8,128)} %rhs_ref.1, s32[31,2,512]{2,1,0:T(2,128)} %map_ref.1, f32[31,512]{1,0:T(8,128)} %coef_ref.1), custom_call_target="tpu_custom_call" | custom-call | tf_op jit(solution)/shard_map/multifrontal/pallas_call | solution.py:459
  179.6 0.0 copy-start.1
  179.6 1.5 copy.10
  181.1 0.0 copy-done.1
  181.1 0.0 copy-start
  181.1 0.6 copy.11
  181.7 0.2 copy-done
  181.8 0.6 copy.12
Async XLA Ops:
  179.6 1.5 copy-start.1
  181.1 0.8 copy-start

commit v4 on v3

--- a/solution.py
+++ b/solution.py
@@ -144,7 +144,7 @@
     diag[...] = a_ref[0:T, 0:T]
     tiles = [slice(0, 256), slice(256, 512), slice(512, 768), slice(768, ROWS)]
 
-    def panel(k):
+    def panel(k, tiles):
         here = pl.ds(pl.multiple_of(k * T, T), T)
         lh, ll = split(li[...])
         for tile in tiles:
@@ -168,7 +168,7 @@
             raw[64 + i : 65 + i, :] = row
 
         eliminate(block[:64], 0, store_upper)
-        panel(jnp.maximum(k - 1, 0))
+        panel(jnp.maximum(k - 1, 0), tiles)
         for tile in (slice(512, 768), slice(768, FRONT)):
             x1[tile, here] = dot_nt(th[tile, :], p_sib[here, :]) + dot_nt(tl[tile, :], p_sib[here, :])
             a_ref[tile, here] = x0[tile, here] + x1[tile, here]
@@ -195,7 +195,7 @@
         return 0
 
     lax.fori_loop(0, 4, block_column, 0)
-    panel(3)
+    panel(3, tiles[2:])
 
 
 def schur(a_ref, vh, vl, item):
@@ -270,11 +270,11 @@
 
     up, down = peers[1], peers[Z_LEN - 1]
 
-    def ring_copy(owner, to, way, step):
+    def ring_copy(owner, to, way, step, half):
         rows = pl.ds(pl.multiple_of(owner * 64, 64), 64)
-        ref = full.at[rows, here[1]]
+        ref = full.at[rows, pl.ds(pl.multiple_of(col * 256 + half * T, T), T)]
         return to_peer(
-            ref, ref, ring_send.at[way, step], ring_recv.at[way, step], (leaf, to, col)
+            ref, ref, ring_send.at[way, step, half], ring_recv.at[way, step, half], (leaf, to, col)
         )
 
     def core_copy(owner, half, n):
@@ -282,7 +282,10 @@
         ref = full.at[rows, pl.ds(pl.multiple_of(half * 256, 256), 256)]
         return to_peer(ref, ref, core_send.at[n], core_recv.at[n], (leaf, row, other))
 
-    sends = [ring_copy(row, up, 0, 0), ring_copy(row, down, 1, 0), core_copy(row, col, 0)]
+    sends = []
+    for half in range(2):
+        sends += [ring_copy(row, up, 0, 0, half), ring_copy(row, down, 1, 0, half)]
+    sends.append(core_copy(row, col, 0))
     for copy in sends:
         copy.start()
     slab_copies = [
@@ -297,13 +300,14 @@
     slab_in[row] = slab_out[row]
     owners = [row]
     for step in range(4):
-        for way, owner, to in ((0, peers[7 - step], up), (1, peers[1 + step], down)):
-            if way == 1 and step == 3:
-                continue
-            ring_copy(owner, to, way, step).wait_recv()
-            if step + 1 < 4 - way:
-                sends.append(ring_copy(owner, to, way, step + 1))
-                sends[-1].start()
+        ways = ((0, peers[7 - step], up), (1, peers[1 + step], down))[: 2 if step < 3 else 1]
+        for half in range(2):
+            for way, owner, to in ways:
+                ring_copy(owner, to, way, step, half).wait_recv()
+                if step + 1 < 4 - way:
+                    sends.append(ring_copy(owner, to, way, step + 1, half))
+                    sends[-1].start()
+        for way, owner, to in ways:
             sends.append(core_copy(owner, col, len(owners)))
             sends[-1].start()
             owners.append(owner)
@@ -492,7 +496,7 @@
             pltpu.VMEM((ROWS, S), BF16),
             pltpu.VMEM((16, S), F32),
             pltpu.VMEM((16, S), F32),
-            dma((2, 4)), dma((2, 4)),
+            dma((2, 4, 2)), dma((2, 4, 2)),
             dma((8,)), dma((8,)),
             dma((8,)), dma((8,)),
             dma((8,)), dma((8,)),

time: 183 us -> 182 us (level)
  no operation moved by 1% of the time
where the time goes in v4:
time: 182 us
  Pallas kernels  179 us (98%)
  local copies, waits for them, and re-layouts  2.87 us (2%)
    pallas_call x1, Pallas kernels, per_device(): pl.pallas_call(kernel, name='multifrontal', out_shape=(jax.ShapeDtypeStru...  179 us

profile of v4, /device:TPU:1, one launch (start us, length us, event | category | flops | bytes accessed | tf_op | source)
XLA Modules:
  0.0 182.1 jit_solution(8571174580959300651)
XLA Ops:
  0.6 178.6 %multifrontal.1 = (f32[64,256]{1,0:T(8,128)}, f32[64,128]{1,0:T(8,128)}, f32[1,64,128]{2,1,0:T(8,128)}) custom-call(f32[1,64,256]{2,1,0:T(8,128)} %upd_ref.1, f32[1,64,128]{2,1,0:T(8,128)} %rhs_ref.1, s32[31,2,512]{2,1,0:T(2,128)} %map_ref.1, f32[31,512]{1,0:T(8,128)} %coef_ref.1), custom_call_target="tpu_custom_call" | custom-call | tf_op jit(solution)/shard_map/multifrontal/pallas_call | solution.py:463
  179.3 0.0 copy-start.1
  179.3 1.5 copy.10
  180.7 0.0 copy-done.1
  180.7 0.0 copy-start
  180.7 0.6 copy.11
  181.4 0.2 copy-done
  181.5 0.6 copy.12
Async XLA Ops:
  179.3 1.5 copy-start.1
  180.7 0.8 copy-start
